TPU v7x, 32 devices: a whole 2x2x4 slice. The times are simulated.
32 devices in a mesh: parts: 2 (over x), sta: 16 (over z, y, core).
Axes of the slice: x: 2, y: 2, z: 4, core: 2. Of those that a mesh axis runs over, the one named last changes fastest.
Arguments:
- data: bfloat16 [32, 3, 896], P(('parts', 'sta')), parts along dimension 0, may hold values from -40 to 40
- templates: bfloat16 [128, 3, 512], P('sta'), may hold values from -12 to 12
- station_lists: int32 [16, 128], replicated, may hold values from 0 to 15, as said below
- counts: int32 [128], replicated, may hold values from 8 to 16
- offsets: int32 [16, 128], replicated, may hold values from 0 to 127
Outputs:
- detection: float32 [256, 256], P(('parts', 'sta')), parts along dimension 0
There are 2 independent parts, one for each index of `parts`. A program takes and returns all parts, laid end to end along the dimension named above; an argument that names none is the same for every part. Nothing has to cross between parts.
Inputs may be any that keep to these rules, and one draw needn't show every extreme that they name: `station_lists`: each column names every one of the 16 stations once; template t uses the stations in entries k < counts[t] of its column. offsets[k, t] belongs to the station in entry k of template t's column.
All inputs are finite; a program needn't handle non-finite values.
Results may differ from a plain program's by a relative error of at most 0.0028.
Values may be sent and summed in bfloat16 or wider, within the bound.
A program may use at most 64 MiB of HBM per device.

v0:
```python
import math

import jax
import jax.numpy as jnp
from jax import lax
from jax.sharding import PartitionSpec as P

NCH = 3
L = 512
NTAU = 256


def center_templates(templates):
    values = templates.astype(jnp.float32)
    return (values - jnp.mean(values, axis=2, keepdims=True)).astype(jnp.bfloat16)


def template_scale(centered):
    values = centered.astype(jnp.float32)
    return jnp.sqrt(jnp.mean(values * values, axis=2) + 1e-06)


def sample_blocks(samples, lag_count):
    item_count, channel_count, length = samples.shape
    width = length - lag_count
    block_count = lag_count // 128
    reshaped = samples.reshape(item_count, channel_count, length // 128, 128)
    return jnp.concatenate(
        [
            reshaped[:, :, step_index : step_index + block_count]
            for step_index in range(width // 128 + 1)
        ],
        axis=3,
    )


def window_scale(blocks, width):
    block_span = blocks.shape[3]
    column = lax.broadcasted_iota(jnp.int32, (block_span, 128), 0)
    lane_index = lax.broadcasted_iota(jnp.int32, (block_span, 128), 1)
    window = ((column >= lane_index) & (column < lane_index + width)).astype(jnp.float32)
    values = blocks.astype(jnp.float32)
    window_sum = jnp.einsum("scbj,jr->scbr", values, window, precision=lax.Precision.HIGHEST)
    square_sum = jnp.einsum(
        "scbj,jr->scbr", values * values, window, precision=lax.Precision.HIGHEST
    )
    out_shape = (blocks.shape[0], blocks.shape[1], blocks.shape[2] * 128)
    mean_one = window_sum.reshape(out_shape) / width
    mean_two = square_sum.reshape(out_shape) / width
    return jnp.sqrt(mean_two - mean_one * mean_one + 1e-05)


def link_tables(station_lists, counts, offsets, width):
    listed = station_lists.shape[0]
    wanted = lax.broadcasted_iota(jnp.int32, (1, 1, width), 2)
    in_count = lax.broadcasted_iota(jnp.int32, (listed, 1, 1), 0) < counts[None, :, None]
    matches = (station_lists[:, :, None] == wanted) & in_count
    member = jnp.any(matches, axis=0).astype(jnp.float32)
    shifts = jnp.sum(jnp.where(matches, offsets[:, :, None], 0), axis=0)
    return (member, shifts)


def stack_rows(fitted, member, shifts, lags_out):
    current = fitted
    bit_count = (fitted.shape[2] - lags_out - 1).bit_length()
    for bit_number in reversed(range(bit_count)):
        shift_step = 1 << bit_number
        kept_width = current.shape[2] - shift_step
        chosen = shifts >> bit_number & 1 == 1
        current = jnp.where(
            chosen[:, :, None], current[:, :, shift_step:], current[:, :, :kept_width]
        )
    return jnp.sum(member[:, :, None] * current[:, :, :lags_out], axis=1)


def body(data, templates, station_lists, counts, offsets):
    lag_count = data.shape[2] - L
    centered = center_templates(templates)
    own_templates = templates.shape[0]
    own_first = lax.axis_index("sta") * own_templates
    own_lists = lax.dynamic_slice_in_dim(station_lists, own_first, own_templates, 1)
    own_counts = lax.dynamic_slice_in_dim(counts, own_first, own_templates, 0)
    own_offsets = lax.dynamic_slice_in_dim(offsets, own_first, own_templates, 1)
    samples_all = lax.all_gather(data, "sta", axis=0, tiled=True)
    station_total = samples_all.shape[0]
    member, shifts = link_tables(own_lists, own_counts, own_offsets, station_total)
    chan_norms = template_scale(centered)
    block_span = L + 128
    padded = jnp.pad(centered, ((0, 0), (0, 0), (0, 129)))
    repeated = jnp.tile(padded, (1, 1, 128))
    toeplitz = repeated[:, :, : 128 * block_span].reshape(own_templates, NCH, 128, block_span)
    toeplitz = jnp.transpose(toeplitz, (1, 3, 0, 2)).reshape(NCH, block_span, own_templates * 128)
    group_size = math.gcd(station_total, 64)

    def add_stations(step_index, running):
        blocks = sample_blocks(samples_all, lag_count)
        scales = window_scale(blocks, L)
        block_count = blocks.shape[2]
        products = jnp.einsum(
            "scbj,cjq->scbq", blocks, toeplitz, preferred_element_type=jnp.float32
        )
        products = products.reshape(group_size, NCH, block_count, own_templates, 128)
        products = jnp.transpose(products, (3, 0, 1, 2, 4)).reshape(
            own_templates, group_size, NCH, block_count * 128
        )
        normalized = products / (L * chan_norms[:, None, :, None] * scales[None])
        fitted = jnp.sum(normalized, axis=2) / NCH
        return running + stack_rows(fitted, member, shifts, NTAU)

    zero_rows = jnp.zeros((own_templates, NTAU), jnp.float32)
    return lax.fori_loop(0, station_total // group_size, add_stations, zero_rows)


def solution(mesh):
    placed = (P(("parts", "sta"), None, None), P("sta", None, None), P(), P(), P())
    return jax.shard_map(
        body, mesh=mesh, in_specs=placed, out_specs=P(("parts", "sta"), None), check_vma=False
    )
```

profile of v0, /device:TPU:0, one launch (start us, length us, event | category | flops | bytes accessed | tf_op | source)
XLA Modules:
  0.0 48.1 jit_solution(976873297776806663)
XLA Ops:
  0.0 0.8 %convert_reduce_fusion = f32[8,3]{0,1:T(4,128)S(1)} fusion(bf16[8,3,512]{2,0,1:T(8,128)(2,1)} %param.6), kind=kLoop, calls=%fused_computation.32 | loop fusion | flops 24552 | bytes 24672 | tf_op jit(solution)/shard_map/reduce_sum | solution.py:15
  0.8 0.9 %multiply_reduce_fusion = (f32[8,3]{0,1:T(4,128)S(1)}, bf16[8,3,512]{2,0,1:T(8,128)(2,1)S(1)}) fusion(f32[8,3]{0,1:T(4,128)S(1)} %broadcast_multiply_fusion.1, bf16[8,3,512]{2,0,1:T(8,128)(2,1)} %param.6), kind=kLoop, calls=%fused_computation.34 | loop fusion | flops 73704 | bytes 49344 | tf_op jit(solution)/shard_map/reduce_sum | solution.py:20
  1.7 2.4 %tile.4 = bf16[8,3,128,641]{3,2,0,1:T(8,128)(2,1)} broadcast(bf16[8,3,641]{2,0,1:T(8,128)(2,1)S(1)} %pad.4), dimensions={0,1,3} | broadcast | bytes 3969072 | tf_op jit(solution)/shard_map/tile | solution.py:90
  4.2 8.7 %tile.10 = bf16[8,3,82048]{2,0,1:T(8,128)(2,1)} reshape(bf16[8,3,128,641]{3,2,0,1:T(8,128)(2,1)} %tile.4) | data formatting | bytes 7876608 | tf_op jit(solution)/shard_map/tile | solution.py:90
  12.9 0.0 slice-start
  12.9 2.1 %slice-done = bf16[8,3,81920]{2,0,1:T(8,128)(2,1)S(1)} async-done(((bf16[8,3,82048]{2,0,1:T(8,128)(2,1)}), bf16[8,3,81920]{2,0,1:T(8,128)(2,1)S(1)}, s32[]{:S(2)}) %slice-start) | async-done | bytes 3932184 | tf_op jit(solution)/shard_map/slice | solution.py:91
  15.0 0.0 copy-start.2
  15.0 2.6 %copy.54 = bf16[3,8,128,640]{3,2,1,0:T(8,128)(2,1)} copy(bf16[3,8,128,640]{3,1,2,0:T(8,128)(2,1)S(1)} %bitcast.41) | data formatting | bytes 7864320
  17.6 0.0 copy-done.2
  17.6 23.4 %all_gather.3 = bf16[16,3,896]{2,1,0:T(4,128)(2,1)S(1)} all-gather(bf16[1,3,896]{2,1,0:T(4,128)(2,1)S(1)} %copy-done.2), channel_id=1, replica_groups=mesh['parts'=2,'sta'=16] {'sta'}, dimensions={0}, use_global_device_ids=true | all-gather | bytes 91392 | tf_op jit(solution)/shard_map/all_gather | solution.py:84
  40.9 0.1 reshape.121
  41.0 0.1 fusion.20
  41.2 0.0 copy-start
  41.2 0.0 copy-start.1
  41.3 0.0 copy-start.3
  41.3 3.4 %fusion.21 = f32[3,1024,16,3]{1,2,3,0:T(8,128)S(1)} fusion(bf16[3,640,1024,1]{1,2,3,0:T(8,128)(2,1)} %bitcast.40, bf16[16,3,3,640]{3,0,2,1:T(8,128)(2,1)S(1)} %copy_dynamic-update-slice_fusion), kind=kOutput, calls=%fused_computation.55 | convolution fusion | flops 188743680 | bytes 4706304 | tf_op jit(solution)/shard_map/while/body/eval_jaxpr/scbj,cjq->scbq/dot_general | solution.py:99
  44.7 0.1 copy.47
  44.8 0.4 convolution_multiply_fusion.1
  45.2 0.3 fusion.3
  45.5 0.2 fusion.4
  45.7 0.1 copy.29
  45.8 0.1 div.31
  45.9 0.0 copy-done
  45.9 0.0 copy-done.1
  45.9 0.1 constant_dynamic-slice_fusion
  46.0 0.0 copy-done.3
  46.0 0.1 dynamic_slice.10
  46.1 0.1 select_reduce_fusion
  46.3 0.1 slice_select_fusion.5
  46.4 0.1 slice_select_fusion.4
  46.5 0.1 slice_select_fusion.3
  46.7 0.1 slice_select_fusion.2
  46.8 0.1 slice_select_fusion.1
  47.0 0.1 slice_select_fusion
  47.1 0.1 fusion.19
  47.2 0.1 fusion.16
  47.4 0.7 %fusion.14 = f32[8,256]{1,0:T(8,128)} fusion(f32[8,16,257]{2,1,0:T(8,128)S(1)} %get-tuple-element.20, f32[8,16,257]{2,1,0:T(8,128)S(1)} %get-tuple-element.19, f32[8,16]{1,0:T(8,128)S(1)} %convert_element_type.24, pred[8,16]{1,0:T(8,128)(4,1)S(1)} %get-tuple-element.35), kind=kLoop, calls=%fused_computation.25 | loop fusion | flops 96256 | bytes 270976 | tf_op jit(solution)/shard_map/while/body/eval_jaxpr/reduce_sum | solution.py:73
  (13 shorter events, 0.1 us)
Async XLA Ops:
  12.9 2.1 %slice-start = ((bf16[8,3,82048]{2,0,1:T(8,128)(2,1)}), bf16[8,3,81920]{2,0,1:T(8,128)(2,1)S(1)}, s32[]{:S(2)}) async-start(bf16[8,3,82048]{2,0,1:T(8,128)(2,1)} %tile.10), calls=%async_computation | async-start | bytes 7864320 | tf_op jit(solution)/shard_map/slice | solution.py:91
  15.0 2.6 %copy-start.2 = (bf16[1,3,896]{2,1,0:T(4,128)(2,1)S(1)}, bf16[1,3,896]{2,1,0:T(4,128)(2,1)}, u32[]{:S(2)}) copy-start(bf16[1,3,896]{2,1,0:T(4,128)(2,1)} %param.5) | copy-start | bytes 16132
  41.2 4.7 %copy-start = (s32[16,128]{1,0:T(8,128)S(1)}, s32[16,128]{1,0:T(8,128)}, u32[]{:S(2)}) copy-start(s32[16,128]{1,0:T(8,128)} %param.9) | copy-start | bytes 24580
  41.2 4.7 %copy-start.1 = (s32[16,128]{1,0:T(8,128)S(1)}, s32[16,128]{1,0:T(8,128)}, u32[]{:S(2)}) copy-start(s32[16,128]{1,0:T(8,128)} %param.7) | copy-start | bytes 24580
  41.3 4.8 %copy-start.3 = (s32[128]{0:T(128)S(1)}, s32[128]{0:T(128)}, u32[]{:S(2)}) copy-start(s32[128]{0:T(128)} %param.8) | copy-start | bytes 1540
where the time goes:
time: 48.4 us; the launch traced here: 48.1 us
  blocking collectives  23.4 us (48%)
  local copies, waits for them, and re-layouts  16.7 us (35%)
  matrix products  4.02 us (8%)
  other arithmetic  3.7 us (8%)
    all_gather x1, blocking collectives, body(): samples_all = lax.all_gather(data, 'sta', axis=0, tiled=True)  23.4 us
    another operation x2, local copies, waits for them, and re-layouts, body(): repeated = jnp.tile(padded, (1, 1, 128))  11.2 us
    dot_general x1, matrix products, add_stations(): jnp.einsum('scbj,cjq->scbq', blocks, toeplitz, preferred_element_type=jnp...  3.4 us
    unnamed x14, local copies, waits for them, and re-layouts  2.75 us
    slice x2, local copies, waits for them, and re-layouts, body(): repeated[:, :, :128 * block_span]  2.11 us

commit v1 on v0

v1 whole, which is shorter than its diff:
```python
import functools

import jax
import jax.numpy as jnp
from jax import lax
from jax.experimental import pallas as pl
from jax.experimental.pallas import tpu as pltpu
from jax.sharding import PartitionSpec as P

NCH = 3
L = 512
NTAU = 256
LANES = 128
SLOT = 24
F32 = jnp.float32
MESH = pl.DeviceIdType.MESH


def dot_nt(a, b):
    return lax.dot_general(a, b, (((1,), (1,)), ((), ())), preferred_element_type=F32)


def network_kernel(
    n, data_ref, templates_ref, lists_ref, counts_ref, offsets_ref, out_ref,
    slots, bands, send_sem, recv_sem,
):
    me = lax.axis_index("sta")
    samples_len = data_ref.shape[2]
    blocks = samples_len // LANES
    lag_blocks = (samples_len - L) // LANES
    out_blocks = NTAU // LANES
    wave_blocks = L // LANES
    span = L + LANES
    own = templates_ref.shape[1]

    barrier = pltpu.get_barrier_semaphore()

    @pl.loop(1, n)
    def greet(step):
        pl.semaphore_signal(
            barrier, inc=1, device_id={"sta": lax.rem(me + step, n)}, device_id_type=MESH
        )

    first_row = pl.multiple_of(me * SLOT, 8)
    own_samples = data_ref[0].astype(F32)
    rows = [own_samples[:, LANES * b : LANES * (b + 1)] for b in range(blocks)]
    rows.append(jnp.zeros((SLOT - NCH * blocks, LANES), F32))
    slots[pl.ds(first_row, SLOT), :] = jnp.concatenate(rows, axis=0)

    pl.semaphore_wait(barrier, n - 1)

    def copy_to(step):
        peer = lax.rem(me + step, n)
        return pltpu.make_async_remote_copy(
            src_ref=slots.at[pl.ds(first_row, SLOT), :],
            dst_ref=slots.at[pl.ds(first_row, SLOT), :],
            send_sem=send_sem.at[step],
            recv_sem=recv_sem.at[step],
            device_id={"sta": peer},
            device_id_type=MESH,
        )

    @pl.loop(1, n)
    def send(step):
        copy_to(step).start()

    row_id = lax.broadcasted_iota(jnp.int32, (LANES, LANES), 0)
    lane_id = lax.broadcasted_iota(jnp.int32, (LANES, LANES), 1)
    upper = lane_id >= row_id
    zeros = jnp.zeros((LANES, LANES), F32)
    factors = []
    for c in range(NCH):
        values = templates_ref[c].astype(F32)
        mean = jnp.sum(values, axis=1, keepdims=True) / L
        centered = (values - mean).astype(jnp.bfloat16).astype(F32)
        power = jnp.sum(centered * centered, axis=1, keepdims=True) / L
        factors.append(1.0 / (NCH * L * jnp.sqrt(power + 1e-06)))
        for t in range(own):
            before = zeros
            for k in range(wave_blocks + 1):
                if k < wave_blocks:
                    row = centered[t : t + 1, LANES * k : LANES * (k + 1)]
                    turned = pltpu.roll(
                        jnp.broadcast_to(row, (LANES, LANES)), 0, 1, stride=1, stride_axis=0
                    )
                else:
                    turned = zeros
                bands[c, LANES * t : LANES * (t + 1), LANES * k : LANES * (k + 1)] = jnp.where(
                    upper, turned, before
                ).astype(jnp.bfloat16)
                before = turned

    width = counts_ref.shape[1]
    station = lax.broadcasted_iota(jnp.int32, (n, width), 0)
    lane = lax.broadcasted_iota(jnp.int32, (n, width), 1)
    counts = counts_ref[...]
    table = jnp.zeros((n, width), jnp.int32)
    for k in range(lists_ref.shape[0]):
        match = (lists_ref[k : k + 1, :] == station) & (k < counts)
        table = table + jnp.where(match, offsets_ref[k : k + 1, :] + 256, 0)
    table = table.astype(F32)
    codes = [
        jnp.sum(jnp.where(lane == me * own + t, table, 0.0), axis=1, keepdims=True).astype(jnp.int32)
        for t in range(own)
    ]

    window_row = lax.broadcasted_iota(jnp.int32, (span, LANES), 0)
    window_lane = lax.broadcasted_iota(jnp.int32, (span, LANES), 1)
    window = ((window_row >= window_lane) & (window_row < window_lane + L)).astype(F32)
    window = window.astype(jnp.bfloat16)

    @pl.loop(1, n)
    def receive(step):
        sender = lax.rem(me - step + n, n)
        landed = slots.at[pl.ds(pl.multiple_of(sender * SLOT, 8), SLOT), :]
        pltpu.make_async_remote_copy(
            src_ref=landed,
            dst_ref=landed,
            send_sem=send_sem.at[step],
            recv_sem=recv_sem.at[step],
            device_id={"sta": sender},
            device_id_type=MESH,
        ).wait_recv()

    def spread(parts):
        return jnp.concatenate(
            [
                jnp.concatenate(parts[b : b + wave_blocks + 1], axis=1)
                for b in range(lag_blocks)
            ],
            axis=0,
        )

    held = lag_blocks * n
    operands, squares = [], []
    for c in range(NCH):
        parts = [slots[pl.ds(NCH * b + c, n, stride=SLOT), :] for b in range(blocks)]
        operands.append(spread([x.astype(jnp.bfloat16) for x in parts]))
        high = [(x * x).astype(jnp.bfloat16) for x in parts]
        low = [(x * x - h.astype(F32)).astype(jnp.bfloat16) for x, h in zip(parts, high)]
        squares.append((spread(high), spread(low)))
    fitted = [None] * own
    for c in range(NCH):
        stacked = jnp.concatenate([operands[c], *squares[c]], axis=0)
        sums = jnp.dot(stacked, window, preferred_element_type=F32)
        mean_one = sums[:held] / L
        mean_two = (sums[held : 2 * held] + sums[2 * held :]) / L
        inverse = 1.0 / jnp.sqrt(mean_two - mean_one * mean_one + 1e-05)
        products = dot_nt(operands[c], bands[c])
        for t in range(own):
            term = products[:, LANES * t : LANES * (t + 1)] * (inverse * factors[c][t : t + 1, :])
            fitted[t] = term if c == 0 else fitted[t] + term

    lane = lax.broadcasted_iota(jnp.int32, (n, LANES), 1)
    for t in range(own):
        code = jnp.broadcast_to(codes[t], (n, LANES))
        shift = code & 127
        member = code >= 256
        tiled = jnp.concatenate([shift] * lag_blocks, axis=0)
        current = fitted[t]
        for bit in range(7):
            step = 1 << bit
            current = jnp.where(
                (tiled & step) != 0, pltpu.roll(current, LANES - step, 1), current
            )
        stays = lane + shift < LANES
        for b in range(out_blocks):
            picked = jnp.where(
                stays, current[n * b : n * (b + 1)], current[n * (b + 1) : n * (b + 2)]
            )
            out_ref[t : t + 1, LANES * b : LANES * (b + 1)] = jnp.sum(
                jnp.where(member, picked, 0.0), axis=0, keepdims=True
            )

    @pl.loop(1, n)
    def sent(step):
        copy_to(step).wait_send()


def body(n, data, templates, station_lists, counts, offsets):
    own, _, length = templates.shape
    return pl.pallas_call(
        functools.partial(network_kernel, n),
        out_shape=jax.ShapeDtypeStruct((own, NTAU), F32),
        in_specs=[pl.BlockSpec(memory_space=pltpu.VMEM)] * 5,
        out_specs=pl.BlockSpec(memory_space=pltpu.VMEM),
        scratch_shapes=[
            pltpu.VMEM((n * SLOT, LANES), F32),
            pltpu.VMEM((NCH, own * LANES, length + LANES), jnp.bfloat16),
            pltpu.SemaphoreType.DMA((n,)),
            pltpu.SemaphoreType.DMA((n,)),
        ],
        compiler_params=pltpu.CompilerParams(
            collective_id=0, has_side_effects=True, vmem_limit_bytes=40 * 1024 * 1024
        ),
    )(data, jnp.transpose(templates, (1, 0, 2)), station_lists, counts[None, :], offsets)


def solution(mesh):
    placed = (P(("parts", "sta"), None, None), P("sta", None, None), P(), P(), P())
    return jax.shard_map(
        functools.partial(body, mesh.shape["sta"]), mesh=mesh, in_specs=placed,
        out_specs=P(("parts", "sta"), None), check_vma=False,
    )
```

time: 48.4 us -> 16.5 us (0.34)
  blocking collectives: 23.4 us -> 0 us
  local copies, waits for them, and re-layouts: 16.7 us -> 4.08 us
  Pallas kernels: 0 us -> 12.1 us
  matrix products: 4.02 us -> 0 us
  other arithmetic: 3.7 us -> 0 us
    all_gather x1 -> x0, blocking collectives: 23.4 us -> none  [body(): samples_all = lax.all_gather(data, 'sta', axis=0, tiled=True)]
    pallas_call x0 -> x1, Pallas kernels: none -> 12.1 us  [body(): pl.pallas_call(functools.partial(network_kernel, n), out_shape=jax.ShapeD...]
    another operation x2 -> x0, local copies, waits for them, and re-layouts: 11.2 us -> none  [body(): repeated = jnp.tile(padded, (1, 1, 128))]
    dot_general x3 -> x0, matrix products: 4.02 us -> none  [the longest x1 3.4 us: add_stations(): jnp.einsum('scbj,cjq->scbq', blocks, toeplitz, preferred_element_type=jnp...]
    reduce_sum x5 -> x0, other arithmetic: 2.72 us -> none  [the longest x1 0.9 us: template_scale(): return jnp.sqrt(jnp.mean(values * values, axis=2) + 1e-06)]
    slice x4 -> x0, local copies, waits for them, and re-layouts: 2.32 us -> none  [the longest x2 2.11 us: body(): repeated[:, :, :128 * block_span]]
    unnamed x14 -> x11, local copies, waits for them, and re-layouts: 2.75 us -> 4.08 us
    select_n x6 -> x0, other arithmetic: 0.81 us -> none  [stack_rows(): jnp.where(chosen[:, :, None], current[:, :, shift_step:], current[:, :, :...]
where the time goes in v1:
time: 16.5 us; the launch traced here: 16.2 us
  Pallas kernels  12.1 us (73%)
  local copies, waits for them, and re-layouts  4.08 us (25%)
    pallas_call x1, Pallas kernels, body(): pl.pallas_call(functools.partial(network_kernel, n), out_shape=jax.ShapeD...  12.1 us
    unnamed x11, local copies, waits for them, and re-layouts  4.08 us

profile of v1, /device:TPU:0, one launch (start us, length us, event | category | flops | bytes accessed | tf_op | source)
XLA Modules:
  0.0 16.2 jit_solution(11887779575333004223)
XLA Ops:
  0.0 0.0 copy-start.4
  0.0 0.7 %copy-done.4 = s32[128]{0:T(128)S(1)} copy-done((s32[128]{0:T(128)S(1)}, s32[128]{0:T(128)}, u32[]{:S(2)}) %copy-start.4) | copy-done | bytes 536
  0.7 0.0 copy-start
  0.7 0.7 %copy-done = bf16[8,3,512]{2,0,1:T(8,128)(2,1)S(1)} copy-done((bf16[8,3,512]{2,0,1:T(8,128)(2,1)S(1)}, bf16[8,3,512]{2,0,1:T(8,128)(2,1)}, u32[]{:S(2)}) %copy-start) | copy-done | bytes 24600
  1.4 0.0 copy-start.1
  1.4 0.7 %copy-done.1 = s32[16,128]{1,0:T(8,128)S(1)} copy-done((s32[16,128]{1,0:T(8,128)S(1)}, s32[16,128]{1,0:T(8,128)}, u32[]{:S(2)}) %copy-start.1) | copy-done | bytes 8216
  2.1 0.0 copy-start.2
  2.1 0.7 %copy-done.2 = s32[16,128]{1,0:T(8,128)S(1)} copy-done((s32[16,128]{1,0:T(8,128)S(1)}, s32[16,128]{1,0:T(8,128)}, u32[]{:S(2)}) %copy-start.2) | copy-done | bytes 8216
  2.8 0.0 copy-start.3
  2.8 0.7 %copy-done.3 = bf16[1,3,896]{2,1,0:T(4,128)(2,1)S(1)} copy-done((bf16[1,3,896]{2,1,0:T(4,128)(2,1)S(1)}, bf16[1,3,896]{2,1,0:T(4,128)(2,1)}, u32[]{:S(2)}) %copy-start.3) | copy-done | bytes 5400
  3.5 12.1 %shard_map.55 = f32[8,256]{1,0:T(8,128)S(1)} custom-call(bf16[1,3,896]{2,1,0:T(4,128)(2,1)S(1)} %copy-done.3, bf16[3,8,512]{2,1,0:T(8,128)(2,1)S(1)} %bitcast.2, s32[16,128]{1,0:T(8,128)S(1)} %copy-done.1, s32[1,128]{1,0:T(1,128)S(1)} %bitcast.3, s32[16,128]{1,0:T(8,128)S(1)} %copy-done.2), custom_call_target="tpu_custom_call" | custom-call | tf_op jit(solution)/shard_map/pallas_call | solution.py:182
  15.6 0.6 %copy.7 = f32[8,256]{1,0:T(8,128)} copy(f32[8,256]{1,0:T(8,128)S(1)} %shard_map.55) | data formatting | bytes 16384
Async XLA Ops:
  0.0 0.7 %copy-start.4 = (s32[128]{0:T(128)S(1)}, s32[128]{0:T(128)}, u32[]{:S(2)}) copy-start(s32[128]{0:T(128)} %param.8) | copy-start | bytes 1540
  0.7 0.7 %copy-start = (bf16[8,3,512]{2,0,1:T(8,128)(2,1)S(1)}, bf16[8,3,512]{2,0,1:T(8,128)(2,1)}, u32[]{:S(2)}) copy-start(bf16[8,3,512]{2,0,1:T(8,128)(2,1)} %param.6) | copy-start | bytes 73732
  1.4 0.7 %copy-start.1 = (s32[16,128]{1,0:T(8,128)S(1)}, s32[16,128]{1,0:T(8,128)}, u32[]{:S(2)}) copy-start(s32[16,128]{1,0:T(8,128)} %lists_ref.1) | copy-start | bytes 24580
  2.1 0.7 %copy-start.2 = (s32[16,128]{1,0:T(8,128)S(1)}, s32[16,128]{1,0:T(8,128)}, u32[]{:S(2)}) copy-start(s32[16,128]{1,0:T(8,128)} %offsets_ref.1) | copy-start | bytes 24580
  2.8 0.7 %copy-start.3 = (bf16[1,3,896]{2,1,0:T(4,128)(2,1)S(1)}, bf16[1,3,896]{2,1,0:T(4,128)(2,1)}, u32[]{:S(2)}) copy-start(bf16[1,3,896]{2,1,0:T(4,128)(2,1)} %data_ref.1) | copy-start | bytes 16132

commit v2 on v1

--- a/solution.py
+++ b/solution.py
@@ -21,9 +21,21 @@
 
 
 def network_kernel(
-    n, data_ref, templates_ref, lists_ref, counts_ref, offsets_ref, out_ref,
-    slots, bands, send_sem, recv_sem,
+    n, data_hbm, templates_hbm, lists_hbm, counts_hbm, offsets_hbm, out_ref,
+    data_ref, templates_ref, lists_ref, counts_ref, offsets_ref,
+    slots, bands, fetch_sem, send_sem, recv_sem,
 ):
+    fetches = [
+        pltpu.make_async_copy(source, target, fetch_sem.at[i])
+        for i, (source, target) in enumerate(
+            [
+                (data_hbm, data_ref), (templates_hbm, templates_ref), (lists_hbm, lists_ref),
+                (counts_hbm, counts_ref), (offsets_hbm, offsets_ref),
+            ]
+        )
+    ]
+    for fetch in fetches:
+        fetch.start()
     me = lax.axis_index("sta")
     samples_len = data_ref.shape[2]
     blocks = samples_len // LANES
@@ -42,6 +54,7 @@
         )
 
     first_row = pl.multiple_of(me * SLOT, 8)
+    fetches[0].wait()
     own_samples = data_ref[0].astype(F32)
     rows = [own_samples[:, LANES * b : LANES * (b + 1)] for b in range(blocks)]
     rows.append(jnp.zeros((SLOT - NCH * blocks, LANES), F32))
@@ -69,6 +82,7 @@
     upper = lane_id >= row_id
     zeros = jnp.zeros((LANES, LANES), F32)
     factors = []
+    fetches[1].wait()
     for c in range(NCH):
         values = templates_ref[c].astype(F32)
         mean = jnp.sum(values, axis=1, keepdims=True) / L
@@ -90,6 +104,8 @@
                 ).astype(jnp.bfloat16)
                 before = turned
 
+    for fetch in fetches[2:]:
+        fetch.wait()
     width = counts_ref.shape[1]
     station = lax.broadcasted_iota(jnp.int32, (n, width), 0)
     lane = lax.broadcasted_iota(jnp.int32, (n, width), 1)
@@ -179,21 +195,24 @@
 
 def body(n, data, templates, station_lists, counts, offsets):
     own, _, length = templates.shape
+    operands = (data, jnp.transpose(templates, (1, 0, 2)), station_lists, counts[None, :], offsets)
     return pl.pallas_call(
         functools.partial(network_kernel, n),
         out_shape=jax.ShapeDtypeStruct((own, NTAU), F32),
-        in_specs=[pl.BlockSpec(memory_space=pltpu.VMEM)] * 5,
+        in_specs=[pl.BlockSpec(memory_space=pltpu.HBM)] * len(operands),
         out_specs=pl.BlockSpec(memory_space=pltpu.VMEM),
-        scratch_shapes=[
+        scratch_shapes=[pltpu.VMEM(x.shape, x.dtype) for x in operands]
+        + [
             pltpu.VMEM((n * SLOT, LANES), F32),
             pltpu.VMEM((NCH, own * LANES, length + LANES), jnp.bfloat16),
+            pltpu.SemaphoreType.DMA((len(operands),)),
             pltpu.SemaphoreType.DMA((n,)),
             pltpu.SemaphoreType.DMA((n,)),
         ],
         compiler_params=pltpu.CompilerParams(
             collective_id=0, has_side_effects=True, vmem_limit_bytes=40 * 1024 * 1024
         ),
-    )(data, jnp.transpose(templates, (1, 0, 2)), station_lists, counts[None, :], offsets)
+    )(*[pltpu.with_memory_space_constraint(x, pltpu.HBM) for x in operands])
 
 
 def solution(mesh):

time: 16.5 us -> 13.2 us (0.80)
  local copies, waits for them, and re-layouts: 4.08 us -> 0.6 us
  Pallas kernels: 12.1 us -> 12.4 us
    unnamed x11 -> x1, local copies, waits for them, and re-layouts: 4.08 us -> 0.6 us
    pallas_call x1, Pallas kernels: 12.1 us -> 12.4 us  [body(): pl.pallas_call(functools.partial(network_kernel, n), out_shape=jax.ShapeD...]
where the time goes in v2:
time: 13.2 us; the launch traced here: 13 us
  Pallas kernels  12.4 us (94%)
  local copies, waits for them, and re-layouts  0.6 us (5%)
    pallas_call x1, Pallas kernels, body(): pl.pallas_call(functools.partial(network_kernel, n), out_shape=jax.ShapeD...  12.4 us
    unnamed x1, local copies, waits for them, and re-layouts  0.6 us

profile of v2, /device:TPU:0, one launch (start us, length us, event | category | flops | bytes accessed | tf_op | source)
XLA Modules:
  0.0 13.0 jit_solution(9325296893415067338)
XLA Ops:
  0.0 12.4 %shard_map.55 = f32[8,256]{1,0:T(8,128)S(1)} custom-call(bf16[1,3,896]{2,1,0:T(4,128)(2,1)} %data_hbm.1, bf16[3,8,512]{2,1,0:T(8,128)(2,1)} %bitcast.2, s32[16,128]{1,0:T(8,128)} %lists_hbm.1, s32[1,128]{1,0:T(1,128)} %bitcast.3, s32[16,128]{1,0:T(8,128)} %offsets_hbm.1), custom_call_target="tpu_custom_call" | custom-call | tf_op jit(solution)/shard_map/pallas_call | solution.py:199
  12.4 0.6 %copy.7 = f32[8,256]{1,0:T(8,128)} copy(f32[8,256]{1,0:T(8,128)S(1)} %shard_map.55) | data formatting | bytes 16384

commit v3 on v2

--- a/solution.py
+++ b/solution.py
@@ -11,7 +11,7 @@
 L = 512
 NTAU = 256
 LANES = 128
-SLOT = 24
+ROWS = 8
 F32 = jnp.float32
 MESH = pl.DeviceIdType.MESH
 
@@ -22,22 +22,22 @@
 
 def network_kernel(
     n, data_hbm, templates_hbm, lists_hbm, counts_hbm, offsets_hbm, out_ref,
-    data_ref, templates_ref, lists_ref, counts_ref, offsets_ref,
-    slots, bands, fetch_sem, send_sem, recv_sem,
+    templates_ref, lists_ref, counts_ref, offsets_ref,
+    slots, staged, bands, fetch_sem, send_sem, recv_sem,
 ):
+    me = lax.axis_index("sta")
     fetches = [
         pltpu.make_async_copy(source, target, fetch_sem.at[i])
         for i, (source, target) in enumerate(
             [
-                (data_hbm, data_ref), (templates_hbm, templates_ref), (lists_hbm, lists_ref),
+                (data_hbm.at[0], slots.at[me]), (templates_hbm, templates_ref), (lists_hbm, lists_ref),
                 (counts_hbm, counts_ref), (offsets_hbm, offsets_ref),
             ]
         )
     ]
     for fetch in fetches:
         fetch.start()
-    me = lax.axis_index("sta")
-    samples_len = data_ref.shape[2]
+    samples_len = data_hbm.shape[2]
     blocks = samples_len // LANES
     lag_blocks = (samples_len - L) // LANES
     out_blocks = NTAU // LANES
@@ -53,23 +53,15 @@
             barrier, inc=1, device_id={"sta": lax.rem(me + step, n)}, device_id_type=MESH
         )
 
-    first_row = pl.multiple_of(me * SLOT, 8)
-    fetches[0].wait()
-    own_samples = data_ref[0].astype(F32)
-    rows = [own_samples[:, LANES * b : LANES * (b + 1)] for b in range(blocks)]
-    rows.append(jnp.zeros((SLOT - NCH * blocks, LANES), F32))
-    slots[pl.ds(first_row, SLOT), :] = jnp.concatenate(rows, axis=0)
-
     pl.semaphore_wait(barrier, n - 1)
 
     def copy_to(step):
-        peer = lax.rem(me + step, n)
         return pltpu.make_async_remote_copy(
-            src_ref=slots.at[pl.ds(first_row, SLOT), :],
-            dst_ref=slots.at[pl.ds(first_row, SLOT), :],
+            src_ref=data_hbm.at[0],
+            dst_ref=slots.at[me],
             send_sem=send_sem.at[step],
             recv_sem=recv_sem.at[step],
-            device_id={"sta": peer},
+            device_id={"sta": lax.rem(me + step, n)},
             device_id_type=MESH,
         )
 
@@ -125,18 +117,27 @@
     window = ((window_row >= window_lane) & (window_row < window_lane + L)).astype(F32)
     window = window.astype(jnp.bfloat16)
 
+    def stage(sender):
+        samples = slots[sender].astype(F32)
+        for b in range(blocks):
+            first_row = pl.multiple_of(sender * (ROWS * blocks) + ROWS * b, ROWS)
+            staged[pl.ds(first_row, NCH), :] = samples[:, LANES * b : LANES * (b + 1)]
+
+    fetches[0].wait()
+    stage(me)
+
     @pl.loop(1, n)
     def receive(step):
         sender = lax.rem(me - step + n, n)
-        landed = slots.at[pl.ds(pl.multiple_of(sender * SLOT, 8), SLOT), :]
         pltpu.make_async_remote_copy(
-            src_ref=landed,
-            dst_ref=landed,
+            src_ref=data_hbm.at[0],
+            dst_ref=slots.at[sender],
             send_sem=send_sem.at[step],
             recv_sem=recv_sem.at[step],
             device_id={"sta": sender},
             device_id_type=MESH,
         ).wait_recv()
+        stage(sender)
 
     def spread(parts):
         return jnp.concatenate(
@@ -150,7 +151,7 @@
     held = lag_blocks * n
     operands, squares = [], []
     for c in range(NCH):
-        parts = [slots[pl.ds(NCH * b + c, n, stride=SLOT), :] for b in range(blocks)]
+        parts = [staged[pl.ds(ROWS * b + c, n, stride=ROWS * blocks), :] for b in range(blocks)]
         operands.append(spread([x.astype(jnp.bfloat16) for x in parts]))
         high = [(x * x).astype(jnp.bfloat16) for x in parts]
         low = [(x * x - h.astype(F32)).astype(jnp.bfloat16) for x, h in zip(parts, high)]
@@ -201,9 +202,10 @@
         out_shape=jax.ShapeDtypeStruct((own, NTAU), F32),
         in_specs=[pl.BlockSpec(memory_space=pltpu.HBM)] * len(operands),
         out_specs=pl.BlockSpec(memory_space=pltpu.VMEM),
-        scratch_shapes=[pltpu.VMEM(x.shape, x.dtype) for x in operands]
+        scratch_shapes=[pltpu.VMEM(x.shape, x.dtype) for x in operands[1:]]
         + [
-            pltpu.VMEM((n * SLOT, LANES), F32),
+            pltpu.VMEM((n, *data.shape[1:]), data.dtype),
+            pltpu.VMEM((n * ROWS * (data.shape[2] // LANES), LANES), F32),
             pltpu.VMEM((NCH, own * LANES, length + LANES), jnp.bfloat16),
             pltpu.SemaphoreType.DMA((len(operands),)),
             pltpu.SemaphoreType.DMA((n,)),

time: 13.2 us -> 12.4 us (0.939)
  Pallas kernels: 12.4 us -> 11.6 us
    pallas_call x1, Pallas kernels: 12.4 us -> 11.6 us  [body(): pl.pallas_call(functools.partial(network_kernel, n), out_shape=jax.ShapeD...]
where the time goes in v3:
time: 12.4 us; the launch traced here: 12.2 us
  Pallas kernels  11.6 us (94%)
  local copies, waits for them, and re-layouts  0.6 us (5%)
    pallas_call x1, Pallas kernels, body(): pl.pallas_call(functools.partial(network_kernel, n), out_shape=jax.ShapeD...  11.6 us
    unnamed x1, local copies, waits for them, and re-layouts  0.6 us

profile of v3, /device:TPU:0, one launch (start us, length us, event | category | flops | bytes accessed | tf_op | source)
XLA Modules:
  0.0 12.2 jit_solution(17357766304416366617)
XLA Ops:
  0.0 11.6 %shard_map.55 = f32[8,256]{1,0:T(8,128)S(1)} custom-call(bf16[1,3,896]{2,1,0:T(4,128)(2,1)} %data_hbm.1, bf16[3,8,512]{2,1,0:T(8,128)(2,1)} %bitcast.2, s32[16,128]{1,0:T(8,128)} %lists_hbm.1, s32[1,128]{1,0:T(1,128)} %bitcast.3, s32[16,128]{1,0:T(8,128)} %offsets_hbm.1), custom_call_target="tpu_custom_call" | custom-call | tf_op jit(solution)/shard_map/pallas_call | solution.py:200
  11.6 0.6 %copy.7 = f32[8,256]{1,0:T(8,128)} copy(f32[8,256]{1,0:T(8,128)S(1)} %shard_map.55) | data formatting | bytes 16384

commit v4 on v3

--- a/solution.py
+++ b/solution.py
@@ -35,8 +35,7 @@
             ]
         )
     ]
-    for fetch in fetches:
-        fetch.start()
+    fetches[0].start()
     samples_len = data_hbm.shape[2]
     blocks = samples_len // LANES
     lag_blocks = (samples_len - L) // LANES
@@ -47,8 +46,7 @@
 
     barrier = pltpu.get_barrier_semaphore()
 
-    @pl.loop(1, n)
-    def greet(step):
+    for step in range(1, n):
         pl.semaphore_signal(
             barrier, inc=1, device_id={"sta": lax.rem(me + step, n)}, device_id_type=MESH
         )
@@ -57,7 +55,7 @@
 
     def copy_to(step):
         return pltpu.make_async_remote_copy(
-            src_ref=data_hbm.at[0],
+            src_ref=slots.at[me],
             dst_ref=slots.at[me],
             send_sem=send_sem.at[step],
             recv_sem=recv_sem.at[step],
@@ -65,9 +63,11 @@
             device_id_type=MESH,
         )
 
-    @pl.loop(1, n)
-    def send(step):
+    fetches[0].wait()
+    for step in range(1, n):
         copy_to(step).start()
+    for fetch in fetches[1:]:
+        fetch.start()
 
     row_id = lax.broadcasted_iota(jnp.int32, (LANES, LANES), 0)
     lane_id = lax.broadcasted_iota(jnp.int32, (LANES, LANES), 1)
@@ -123,14 +123,14 @@
             first_row = pl.multiple_of(sender * (ROWS * blocks) + ROWS * b, ROWS)
             staged[pl.ds(first_row, NCH), :] = samples[:, LANES * b : LANES * (b + 1)]
 
-    fetches[0].wait()
     stage(me)
 
     @pl.loop(1, n)
-    def receive(step):
-        sender = lax.rem(me - step + n, n)
+    def receive(ahead):
+        step = n - ahead
+        sender = lax.rem(me + ahead, n)
         pltpu.make_async_remote_copy(
-            src_ref=data_hbm.at[0],
+            src_ref=slots.at[sender],
             dst_ref=slots.at[sender],
             send_sem=send_sem.at[step],
             recv_sem=recv_sem.at[step],
@@ -173,13 +173,11 @@
         code = jnp.broadcast_to(codes[t], (n, LANES))
         shift = code & 127
         member = code >= 256
-        tiled = jnp.concatenate([shift] * lag_blocks, axis=0)
-        current = fitted[t]
-        for bit in range(7):
-            step = 1 << bit
-            current = jnp.where(
-                (tiled & step) != 0, pltpu.roll(current, LANES - step, 1), current
-            )
+        turn = (lane + shift) & (LANES - 1)
+        current = jnp.take_along_axis(
+            fitted[t], jnp.concatenate([turn] * lag_blocks, axis=0), axis=1,
+            mode="promise_in_bounds",
+        )
         stays = lane + shift < LANES
         for b in range(out_blocks):
             picked = jnp.where(

time: 12.4 us -> 11.7 us (0.944)
  Pallas kernels: 11.6 us -> 10.9 us
    pallas_call x1, Pallas kernels: 11.6 us -> 10.9 us  [body(): pl.pallas_call(functools.partial(network_kernel, n), out_shape=jax.ShapeD...]
where the time goes in v4:
time: 11.7 us; the launch traced here: 11.5 us
  Pallas kernels  10.9 us (93%)
  local copies, waits for them, and re-layouts  0.6 us (5%)
    pallas_call x1, Pallas kernels, body(): pl.pallas_call(functools.partial(network_kernel, n), out_shape=jax.ShapeD...  10.9 us
    unnamed x1, local copies, waits for them, and re-layouts  0.6 us

profile of v4, /device:TPU:0, one launch (start us, length us, event | category | flops | bytes accessed | tf_op | source)
XLA Modules:
  0.0 11.5 jit_solution(3523486751165264552)
XLA Ops:
  0.0 10.9 %shard_map.55 = f32[8,256]{1,0:T(8,128)S(1)} custom-call(bf16[1,3,896]{2,1,0:T(4,128)(2,1)} %data_hbm.1, bf16[3,8,512]{2,1,0:T(8,128)(2,1)} %bitcast.2, s32[16,128]{1,0:T(8,128)} %lists_hbm.1, s32[1,128]{1,0:T(1,128)} %bitcast.3, s32[16,128]{1,0:T(8,128)} %offsets_hbm.1), custom_call_target="tpu_custom_call" | custom-call | tf_op jit(solution)/shard_map/pallas_call | solution.py:198
  10.9 0.6 %copy.7 = f32[8,256]{1,0:T(8,128)} copy(f32[8,256]{1,0:T(8,128)S(1)} %shard_map.55) | data formatting | bytes 16384

commit v5 on v4

--- a/solution.py
+++ b/solution.py
@@ -16,14 +16,10 @@
 MESH = pl.DeviceIdType.MESH
 
 
-def dot_nt(a, b):
-    return lax.dot_general(a, b, (((1,), (1,)), ((), ())), preferred_element_type=F32)
-
-
 def network_kernel(
     n, data_hbm, templates_hbm, lists_hbm, counts_hbm, offsets_hbm, out_ref,
     templates_ref, lists_ref, counts_ref, offsets_ref,
-    slots, staged, bands, fetch_sem, send_sem, recv_sem,
+    slots, staged, bands, factors_ref, fetch_sem, send_sem, recv_sem,
 ):
     me = lax.axis_index("sta")
     fetches = [
@@ -36,6 +32,7 @@
         )
     ]
     fetches[0].start()
+    fetches[1].start()
     samples_len = data_hbm.shape[2]
     blocks = samples_len // LANES
     lag_blocks = (samples_len - L) // LANES
@@ -50,6 +47,37 @@
         pl.semaphore_signal(
             barrier, inc=1, device_id={"sta": lax.rem(me + step, n)}, device_id_type=MESH
         )
+
+    row_id = lax.broadcasted_iota(jnp.int32, (LANES, LANES), 0)
+    lane_id = lax.broadcasted_iota(jnp.int32, (LANES, LANES), 1)
+    upper = lane_id >= row_id
+    zeros = jnp.zeros((LANES, LANES), F32)
+
+    def build():
+        fetches[1].wait()
+        for c in range(NCH):
+            values = templates_ref[c].astype(F32)
+            mean = jnp.sum(values, axis=1, keepdims=True) / L
+            centered = (values - mean).astype(jnp.bfloat16).astype(F32)
+            power = jnp.sum(centered * centered, axis=1, keepdims=True) / L
+            factor = 1.0 / (NCH * L * jnp.sqrt(power + 1e-06))
+            factors_ref[c] = jnp.broadcast_to(factor, (own, LANES))
+            for t in range(own):
+                before = zeros
+                for k in range(wave_blocks + 1):
+                    if k < wave_blocks:
+                        row = centered[t : t + 1, LANES * k : LANES * (k + 1)]
+                        turned = pltpu.roll(
+                            jnp.broadcast_to(row, (LANES, LANES)), 0, 1, stride=1, stride_axis=0
+                        )
+                    else:
+                        turned = zeros
+                    bands[c, LANES * k : LANES * (k + 1), LANES * t : LANES * (t + 1)] = (
+                        jnp.where(upper, turned, before).T.astype(jnp.bfloat16)
+                    )
+                    before = turned
+
+    pl.when(me < n // 4)(build)
 
     pl.semaphore_wait(barrier, n - 1)
 
@@ -66,35 +94,9 @@
     fetches[0].wait()
     for step in range(1, n):
         copy_to(step).start()
-    for fetch in fetches[1:]:
+    for fetch in fetches[2:]:
         fetch.start()
-
-    row_id = lax.broadcasted_iota(jnp.int32, (LANES, LANES), 0)
-    lane_id = lax.broadcasted_iota(jnp.int32, (LANES, LANES), 1)
-    upper = lane_id >= row_id
-    zeros = jnp.zeros((LANES, LANES), F32)
-    factors = []
-    fetches[1].wait()
-    for c in range(NCH):
-        values = templates_ref[c].astype(F32)
-        mean = jnp.sum(values, axis=1, keepdims=True) / L
-        centered = (values - mean).astype(jnp.bfloat16).astype(F32)
-        power = jnp.sum(centered * centered, axis=1, keepdims=True) / L
-        factors.append(1.0 / (NCH * L * jnp.sqrt(power + 1e-06)))
-        for t in range(own):
-            before = zeros
-            for k in range(wave_blocks + 1):
-                if k < wave_blocks:
-                    row = centered[t : t + 1, LANES * k : LANES * (k + 1)]
-                    turned = pltpu.roll(
-                        jnp.broadcast_to(row, (LANES, LANES)), 0, 1, stride=1, stride_axis=0
-                    )
-                else:
-                    turned = zeros
-                bands[c, LANES * t : LANES * (t + 1), LANES * k : LANES * (k + 1)] = jnp.where(
-                    upper, turned, before
-                ).astype(jnp.bfloat16)
-                before = turned
+    pl.when(me >= n // 4)(build)
 
     for fetch in fetches[2:]:
         fetch.wait()
@@ -163,9 +165,9 @@
         mean_one = sums[:held] / L
         mean_two = (sums[held : 2 * held] + sums[2 * held :]) / L
         inverse = 1.0 / jnp.sqrt(mean_two - mean_one * mean_one + 1e-05)
-        products = dot_nt(operands[c], bands[c])
+        products = jnp.dot(operands[c], bands[c], preferred_element_type=F32)
         for t in range(own):
-            term = products[:, LANES * t : LANES * (t + 1)] * (inverse * factors[c][t : t + 1, :])
+            term = products[:, LANES * t : LANES * (t + 1)] * (inverse * factors_ref[c, t : t + 1, :])
             fitted[t] = term if c == 0 else fitted[t] + term
 
     lane = lax.broadcasted_iota(jnp.int32, (n, LANES), 1)
@@ -204,7 +206,8 @@
         + [
             pltpu.VMEM((n, *data.shape[1:]), data.dtype),
             pltpu.VMEM((n * ROWS * (data.shape[2] // LANES), LANES), F32),
-            pltpu.VMEM((NCH, own * LANES, length + LANES), jnp.bfloat16),
+            pltpu.VMEM((NCH, length + LANES, own * LANES), jnp.bfloat16),
+            pltpu.VMEM((NCH, own, LANES), F32),
             pltpu.SemaphoreType.DMA((len(operands),)),
             pltpu.SemaphoreType.DMA((n,)),
             pltpu.SemaphoreType.DMA((n,)),

time: 11.7 us -> 11.2 us (0.957)
  Pallas kernels: 10.9 us -> 10.4 us
    pallas_call x1, Pallas kernels: 10.9 us -> 10.4 us  [body(): pl.pallas_call(functools.partial(network_kernel, n), out_shape=jax.ShapeD...]
where the time goes in v5:
time: 11.2 us; the launch traced here: 11 us
  Pallas kernels  10.4 us (93%)
  local copies, waits for them, and re-layouts  0.6 us (5%)
    pallas_call x1, Pallas kernels, body(): pl.pallas_call(functools.partial(network_kernel, n), out_shape=jax.ShapeD...  10.4 us
    unnamed x1, local copies, waits for them, and re-layouts  0.6 us

profile of v5, /device:TPU:0, one launch (start us, length us, event | category | flops | bytes accessed | tf_op | source)
XLA Modules:
  0.0 11.0 jit_solution(13593243283863319665)
XLA Ops:
  0.0 10.4 %shard_map.55 = f32[8,256]{1,0:T(8,128)S(1)} custom-call(bf16[1,3,896]{2,1,0:T(4,128)(2,1)} %data_hbm.1, bf16[3,8,512]{2,1,0:T(8,128)(2,1)} %bitcast.2, s32[16,128]{1,0:T(8,128)} %lists_hbm.1, s32[1,128]{1,0:T(1,128)} %bitcast.3, s32[16,128]{1,0:T(8,128)} %offsets_hbm.1), custom_call_target="tpu_custom_call" | custom-call | tf_op jit(solution)/shard_map/pallas_call | solution.py:200
  10.4 0.6 %copy.7 = f32[8,256]{1,0:T(8,128)} copy(f32[8,256]{1,0:T(8,128)S(1)} %shard_map.55) | data formatting | bytes 16384
